TPU v7x, 128 devices: a whole 4x4x4 slice. The times are simulated.
128 devices in a mesh: dp: 64 (over z, y, x), fsdp: 2 (over core).
Axes of the slice: x: 4, y: 4, z: 4, core: 2. Of those that a mesh axis runs over, the one named last changes fastest.
Arguments:
- tokens: bfloat16 [64, 157, 1408], P('dp', None, 'fsdp'), may hold values from -16 to 16
- vis_index: int32 [64, 157], P('dp'), may hold values from 0 to 1567, as said below
- owner: int32 [64, 1568], P('dp'), may hold values from 0 to 1, as said below
- enc_gain: bfloat16 [1408], replicated, may hold values from 0.5 to 1.5
- enc_qkv: bfloat16 [1408, 3, 1408], P(None, None, 'fsdp')
- enc_proj: bfloat16 [1408, 1408], P('fsdp'), may hold values from -0.15625 to 0.15625
- to_decoder: bfloat16 [1408, 512], replicated, may hold values from -0.15625 to 0.15625
- mask_token: bfloat16 [512], replicated, may hold values from -4 to 4
- dec_gain1: bfloat16 [512], replicated, may hold values from 0.5 to 1.5
- dec_qkv: bfloat16 [512, 768], replicated
- dec_proj: bfloat16 [256, 512], replicated, may hold values from -0.375 to 0.375
- dec_gain2: bfloat16 [512], replicated, may hold values from 0.5 to 1.5
- dec_fc1: bfloat16 [512, 2048], replicated, may hold values from -0.25 to 0.25
- dec_fc2: bfloat16 [2048, 512], replicated, may hold values from -0.125 to 0.125
- cotangent: bfloat16 [64, 1568, 512], P('dp', 'fsdp'), may hold values from -0.796875 to 0.796875
Outputs:
- grad_tokens: float32 [64, 157, 1408], P('dp', None, 'fsdp')
- grad_qkv: float32 [1408, 3, 1408], P('dp', None, 'fsdp')
- grad_proj: float32 [1408, 1408], P('fsdp', 'dp')
Inputs may be any that keep to these rules, and one draw needn't show every extreme that they name: `vis_index`: each clip's row is strictly increasing. `owner`: in every clip's row each index of fsdp appears exactly 784 times.
All inputs are finite; a program needn't handle non-finite values.
Results may differ from a plain program's by a relative error of at most 0.02.
Values may be sent and summed in bfloat16 or wider, within the bound.
A program may use at most 192 MiB of HBM per device.

v0:
```python
import math

import jax
import jax.numpy as jnp
from jax import lax
from jax.sharding import PartitionSpec as P

D = 1408
HD = 88
DD = 512
DHD = 64
DH = 4
DI = 256
TUBES = 1568
VIS = 157


EPS = 1e-06
SQRT_HALF = 0.7071067811865476
INV_SQRT_TWO_PI = 0.3989422804014327


def norm_rows(values, gain_row):
    row_mean = jnp.mean(values, axis=-1, keepdims=True)
    centred = values - row_mean
    inv_scale = lax.rsqrt(jnp.mean(centred * centred, axis=-1, keepdims=True) + EPS)
    normed = centred * inv_scale
    return (normed * gain_row, normed, inv_scale)


def norm_rows_back(grad_out, normed, inv_scale, gain_row):
    scaled = grad_out * gain_row
    first_mean = jnp.mean(scaled, axis=-1, keepdims=True)
    second_mean = jnp.mean(scaled * normed, axis=-1, keepdims=True)
    return inv_scale * (scaled - first_mean - normed * second_mean)


def gelu_slope(values):
    return (
        0.5 * (1.0 + lax.erf(values * SQRT_HALF))
        + values * jnp.exp(-0.5 * values * values) * INV_SQRT_TWO_PI
    )


def position_table(tube_ids, width):
    half_width = width // 2
    rates = jnp.exp(jnp.arange(half_width, dtype=jnp.float32) * (-2.0 * math.log(10000.0) / width))
    angles = tube_ids.astype(jnp.float32)[..., None] * rates
    return jnp.stack([jnp.sin(angles), jnp.cos(angles)], axis=-1).reshape(tube_ids.shape + (width,))


def per_device(
    tokens,
    vis_index,
    owner,
    enc_gain,
    enc_qkv,
    enc_proj,
    to_decoder,
    mask_token,
    dec_gain1,
    dec_qkv,
    dec_proj,
    dec_gain2,
    dec_fc1,
    dec_fc2,
    cotangent,
):
    fsdp_count = lax.axis_size("fsdp")
    my_slot = lax.axis_index("fsdp")
    group_clips = tokens.shape[0]
    feat_share = tokens.shape[2]
    head_share = enc_qkv.shape[2]
    heads_mine = head_share // HD
    row_count = group_clips * VIS
    gain_enc = enc_gain.astype(jnp.float32)
    enc_scale = HD ** (-0.5)
    full_tokens = lax.all_gather(tokens, "fsdp", axis=2, tiled=True)
    values = full_tokens.astype(jnp.float32)
    gained, normed, inv_scale = norm_rows(values, gain_enc)
    hidden = gained.astype(jnp.bfloat16).reshape(row_count, D)
    local_qkv = enc_qkv.reshape(D, 3 * head_share)
    qkv_rows = jnp.dot(hidden, local_qkv, preferred_element_type=jnp.float32).reshape(
        group_clips, VIS, 3 * head_share
    )
    query_rows = (
        (qkv_rows[..., :head_share] * enc_scale)
        .astype(jnp.bfloat16)
        .reshape(group_clips, VIS, heads_mine, HD)
    )
    key_rows = (
        qkv_rows[..., head_share : 2 * head_share]
        .astype(jnp.bfloat16)
        .reshape(group_clips, VIS, heads_mine, HD)
    )
    value_rows = (
        qkv_rows[..., 2 * head_share :]
        .astype(jnp.bfloat16)
        .reshape(group_clips, VIS, heads_mine, HD)
    )
    enc_scores = jnp.einsum(
        "gqhd,gkhd->ghqk", query_rows, key_rows, preferred_element_type=jnp.float32
    )
    enc_probs = jax.nn.softmax(enc_scores, axis=-1)
    enc_probs_low = enc_probs.astype(jnp.bfloat16)
    mixed_rows = (
        jnp.einsum("ghqk,gkhd->gqhd", enc_probs_low, value_rows, preferred_element_type=jnp.float32)
        .astype(jnp.bfloat16)
        .reshape(row_count, head_share)
    )
    head_terms = jnp.dot(mixed_rows, enc_proj, preferred_element_type=jnp.float32).reshape(
        group_clips, VIS, D
    )
    proj_mine = lax.psum_scatter(head_terms, "fsdp", scatter_dimension=2, tiled=True)
    encoded = (tokens.astype(jnp.float32) + proj_mine).astype(jnp.bfloat16)
    down_rows = lax.dynamic_slice_in_dim(to_decoder, my_slot * feat_share, feat_share, 0)
    lowered_term = jnp.dot(
        encoded.reshape(row_count, feat_share), down_rows, preferred_element_type=jnp.float32
    )
    lowered_sum = lax.psum(lowered_term, "fsdp")
    group_rows = lowered_sum.astype(jnp.bfloat16).reshape(group_clips, VIS, DD)
    own_count = TUBES // fsdp_count
    is_mine = owner == my_slot
    owned_rank = jnp.cumsum(is_mine.astype(jnp.int32), axis=1) - 1
    slot_ids = jnp.arange(own_count, dtype=jnp.int32)
    tube_ids = jnp.arange(TUBES, dtype=jnp.int32)
    picked = is_mine[:, None, :] & (owned_rank[:, None, :] == slot_ids[None, :, None])
    own_tubes = jnp.sum(jnp.where(picked, tube_ids[None, None, :], 0), axis=2)
    hit_table = own_tubes[:, :, None] == vis_index[:, None, :]
    hits_low = hit_table.astype(jnp.bfloat16)
    placed = jnp.einsum("gjr,grc->gjc", hits_low, group_rows, preferred_element_type=jnp.float32)
    covered = jnp.sum(hit_table.astype(jnp.float32), axis=2, keepdims=True)
    mask_row = mask_token.astype(jnp.float32)
    start_rows = (placed + (1.0 - covered) * mask_row + position_table(own_tubes, DD)).astype(
        jnp.bfloat16
    )
    x_start = start_rows.astype(jnp.float32)
    gain_one = dec_gain1.astype(jnp.float32)
    gain_two = dec_gain2.astype(jnp.float32)
    gained_one, normed_one, inv_one = norm_rows(x_start, gain_one)
    attn_in = gained_one.astype(jnp.bfloat16).reshape(-1, DD)
    dec_mix = jnp.dot(attn_in, dec_qkv, preferred_element_type=jnp.float32).reshape(
        group_clips, own_count, 3 * DI
    )
    dec_scale = DHD ** (-0.5)
    dec_query = (
        (dec_mix[..., :DI] * dec_scale)
        .astype(jnp.bfloat16)
        .reshape(group_clips, own_count, DH, DHD)
    )
    dec_keys = dec_mix[..., DI : 2 * DI].astype(jnp.bfloat16)
    dec_values = dec_mix[..., 2 * DI :].astype(jnp.bfloat16)
    key_piece = lax.all_gather(dec_keys, "fsdp", axis=1, tiled=True)
    value_piece = lax.all_gather(dec_values, "fsdp", axis=1, tiled=True)
    width_here = key_piece.shape[1]
    key_heads = key_piece.reshape(group_clips, width_here, DH, DHD)
    score_part = jnp.einsum(
        "gqhd,gkhd->ghqk", dec_query, key_heads, preferred_element_type=jnp.float32
    )
    keys_all = key_piece
    values_all = value_piece
    dec_scores, keys_all, values_all = (score_part, keys_all, values_all)
    row_max = jnp.max(dec_scores, axis=-1, keepdims=True)
    shifted = jnp.exp(dec_scores - row_max)
    row_total = jnp.sum(shifted, axis=-1, keepdims=True)
    dec_probs = shifted / row_total
    dec_probs_low = dec_probs.astype(jnp.bfloat16)
    values_heads = values_all.reshape(group_clips, TUBES, DH, DHD)
    keys_heads = keys_all.reshape(group_clips, TUBES, DH, DHD)
    dec_mixed = (
        jnp.einsum(
            "ghqk,gkhd->gqhd", dec_probs_low, values_heads, preferred_element_type=jnp.float32
        )
        .astype(jnp.bfloat16)
        .reshape(-1, DI)
    )
    after_attn = (
        x_start
        + jnp.dot(dec_mixed, dec_proj, preferred_element_type=jnp.float32).reshape(
            group_clips, own_count, DD
        )
    ).astype(jnp.bfloat16)
    gained_two, normed_two, inv_two = norm_rows(after_attn.astype(jnp.float32), gain_two)
    mlp_in = gained_two.astype(jnp.bfloat16).reshape(-1, DD)
    up_proj = jnp.dot(mlp_in, dec_fc1, preferred_element_type=jnp.float32)
    grad_act = jnp.dot(cotangent.reshape(-1, DD), dec_fc2.T, preferred_element_type=jnp.float32)
    grad_up = (grad_act * gelu_slope(up_proj)).astype(jnp.bfloat16)
    grad_mlp_in = jnp.dot(grad_up, dec_fc1.T, preferred_element_type=jnp.float32).reshape(
        group_clips, own_count, DD
    )
    grad_mid = cotangent.astype(jnp.float32) + norm_rows_back(
        grad_mlp_in, normed_two, inv_two, gain_two
    )
    grad_mid_low = grad_mid.astype(jnp.bfloat16)
    grad_mix = (
        jnp.dot(grad_mid_low.reshape(-1, DD), dec_proj.T, preferred_element_type=jnp.float32)
        .astype(jnp.bfloat16)
        .reshape(group_clips, own_count, DH, DHD)
    )
    grad_probs = jnp.einsum(
        "gqhd,gkhd->ghqk", grad_mix, values_heads, preferred_element_type=jnp.float32
    )
    centre = jnp.sum(dec_probs * grad_probs, axis=-1, keepdims=True)
    grad_scores = (dec_probs * (grad_probs - centre)).astype(jnp.bfloat16)
    grad_query = jnp.einsum(
        "ghqk,gkhd->gqhd", grad_scores, keys_heads, preferred_element_type=jnp.float32
    ).reshape(group_clips, own_count, DI)
    part_keys = jnp.einsum(
        "ghqk,gqhd->gkhd", grad_scores, dec_query, preferred_element_type=jnp.float32
    ).reshape(group_clips, TUBES, DI)
    part_values = jnp.einsum(
        "ghqk,gqhd->gkhd", dec_probs_low, grad_mix, preferred_element_type=jnp.float32
    ).reshape(group_clips, TUBES, DI)
    grad_keys, grad_values = (
        lax.psum_scatter(
            part_keys.astype(jnp.bfloat16), "fsdp", scatter_dimension=1, tiled=True
        ).astype(jnp.float32),
        lax.psum_scatter(
            part_values.astype(jnp.bfloat16), "fsdp", scatter_dimension=1, tiled=True
        ).astype(jnp.float32),
    )
    grad_dec_qkv = jnp.concatenate(
        [grad_query * dec_scale, grad_keys, grad_values], axis=-1
    ).astype(jnp.bfloat16)
    grad_attn_in = jnp.dot(
        grad_dec_qkv.reshape(-1, 3 * DI), dec_qkv.T, preferred_element_type=jnp.float32
    ).reshape(group_clips, own_count, DD)
    grad_start = grad_mid + norm_rows_back(grad_attn_in, normed_one, inv_one, gain_one)
    grad_start_low = grad_start.astype(jnp.bfloat16)
    back_rows = jnp.einsum(
        "gjr,gjc->grc", hits_low, grad_start_low, preferred_element_type=jnp.float32
    )
    grad_lowered = lax.psum(back_rows.astype(jnp.bfloat16), "fsdp")
    grad_encoded = jnp.dot(
        grad_lowered.reshape(row_count, DD), to_decoder.T, preferred_element_type=jnp.float32
    )
    grad_encoded_low = grad_encoded.astype(jnp.bfloat16)
    grad_enc_mix = (
        jnp.dot(grad_encoded_low, enc_proj.T, preferred_element_type=jnp.float32)
        .astype(jnp.bfloat16)
        .reshape(group_clips, VIS, heads_mine, HD)
    )
    enc_grad_probs = jnp.einsum(
        "gqhd,gkhd->ghqk", grad_enc_mix, value_rows, preferred_element_type=jnp.float32
    )
    enc_centre = jnp.sum(enc_probs * enc_grad_probs, axis=-1, keepdims=True)
    enc_grad_scores = (enc_probs * (enc_grad_probs - enc_centre)).astype(jnp.bfloat16)
    grad_enc_query = jnp.einsum(
        "ghqk,gkhd->gqhd", enc_grad_scores, key_rows, preferred_element_type=jnp.float32
    ).reshape(row_count, head_share)
    grad_enc_keys = jnp.einsum(
        "ghqk,gqhd->gkhd", enc_grad_scores, query_rows, preferred_element_type=jnp.float32
    ).reshape(row_count, head_share)
    grad_enc_values = jnp.einsum(
        "ghqk,gqhd->gkhd", enc_probs_low, grad_enc_mix, preferred_element_type=jnp.float32
    ).reshape(row_count, head_share)
    grad_qkv_low = jnp.concatenate(
        [grad_enc_query * enc_scale, grad_enc_keys, grad_enc_values], axis=-1
    ).astype(jnp.bfloat16)
    hidden_terms = jnp.dot(grad_qkv_low, local_qkv.T, preferred_element_type=jnp.float32).reshape(
        group_clips, VIS, D
    )
    grad_hidden = lax.psum(hidden_terms.astype(jnp.bfloat16), "fsdp").astype(jnp.float32)
    grad_full = grad_encoded.reshape(group_clips, VIS, D) + norm_rows_back(
        grad_hidden, normed, inv_scale, gain_enc
    )
    grad_tokens = lax.dynamic_slice_in_dim(grad_full, my_slot * feat_share, feat_share, 2)
    qkv_term = jnp.dot(hidden.T, grad_qkv_low, preferred_element_type=jnp.float32).reshape(
        D, 3, head_share
    )
    proj_term = jnp.dot(mixed_rows.T, grad_encoded_low, preferred_element_type=jnp.float32)
    grad_qkv_out, grad_proj_out = (
        lax.psum_scatter(qkv_term, "dp", scatter_dimension=0, tiled=True),
        lax.psum_scatter(proj_term, "dp", scatter_dimension=1, tiled=True),
    )
    return (grad_tokens, grad_qkv_out, grad_proj_out)


def solution(mesh):
    return jax.shard_map(
        per_device,
        mesh=mesh,
        in_specs=(
            P("dp", None, "fsdp"),
            P("dp", None),
            P("dp", None),
            P(),
            P(None, None, "fsdp"),
            P("fsdp", None),
            P(),
            P(),
            P(),
            P(),
            P(),
            P(),
            P(),
            P(),
            P("dp", "fsdp", None),
        ),
        out_specs=(P("dp", None, "fsdp"), P("dp", None, "fsdp"), P("fsdp", "dp")),
        check_vma=False,
    )
```

profile of v0, /device:TPU:96, one launch (start us, length us, event | category | flops | bytes accessed | tf_op | source)
XLA Modules:
  0.0 531.7 jit_solution(3380775769574373076)
XLA Ops:
  7.2 2.5 copy.104
  9.7 3.0 all_gather.9
  12.7 3.5 copy.105
  16.7 5.9 %fusion.149 = (bf16[1,157,2112]{2,1,0:T(8,128)(2,1)S(1)}, f32[1,157,2112]{2,1,0:T(8,128)}) fusion(bf16[1408,2112]{0,1:T(8,128)(2,1)} %bitcast.176, f32[1408]{0:T(1024)S(1)} %convert_element_type.203, f32[157]{0:T(256)S(1)} %add_rsqrt_fusion.2, f32[157]{0:T(256)S(1)} %broadcast_multiply_fusion.8, bf16[1,157,1408]{2,1,0:T(8,128)(2,1)S(1)} %copy.105), kind=kOutput, calls=%fused_computation.199 | convolution fusion | flops 935177408 | bytes 8385896 | tf_op jit(solution)/shard_map/dot_general | solution.py:83
  30.2 3.0 convolution_bitcast_fusion.1
  33.2 3.7 copy.130
  40.5 2.9 multiply_sine_fusion
  44.7 4.1 copy.111
  48.8 3.4 reshape.845
  52.2 2.7 copy.112
  58.2 2.5 reshape_bitcast_fusion.2
  60.6 2.9 copy.131
  63.5 2.1 fusion.86
  65.7 5.0 all-reduce.14
  73.3 2.3 fusion.155
  76.4 2.5 all_gather.11
  78.9 2.2 copy.115
  84.3 4.3 all_gather.10
  88.6 2.2 copy.113
  90.8 11.2 %fusion.156 = (f32[4,784]{1,0:T(4,128)S(1)}, f32[4,784,1568]{2,1,0:T(8,128)}) fusion(bf16[784,4,64]{0,2,1:T(8,128)(2,1)S(1)} %bitcast.188, bf16[1568,4,64]{0,2,1:T(8,128)(2,1)} %bitcast.179), kind=kOutput, calls=%fused_computation.202 | convolution fusion | flops 639243776 | bytes 20885760 | tf_op jit(solution)/shard_map/sub | solution.py:164
  102.0 8.9 %fusion.55 = bf16[4,64,784]{2,1,0:T(8,128)(2,1)} fusion(bf16[1568,4,64]{0,2,1:T(8,128)(2,1)} %bitcast.195, f32[4,784]{1,0:T(4,128)S(1)} %get-tuple-element.44, bf16[784,4,64]{0,2,1:T(8,128)(2,1)S(1)} %bitcast.189, bf16[1568,4,64]{0,2,1:T(8,128)(2,1)} %bitcast.180), kind=kOutput, calls=%fused_computation.76 | convolution fusion | flops 1273772544 | bytes 2420992 | tf_op jit(solution)/shard_map/ghqk,gkhd->gqhd/dot_general | solution.py:171
  113.4 4.6 fusion.67
  118.0 9.6 %fusion.144 = (f32[784]{0:T(1024)S(1)}, f32[784]{0:T(1024)S(1)}, f32[784,512]{1,0:T(8,128)}) fusion(f32[784]{0:T(1024)S(1)} %add_rsqrt_fusion, f32[784]{0:T(1024)S(1)} %broadcast_multiply_fusion.4, bf16[784,512]{1,0:T(8,128)(2,1)} %copy-done.7, f32[512]{0:T(512)S(1)} %copy-done.31, bf16[512,2048]{1,0:T(8,128)(2,1)S(1)} %copy-done, ...), kind=kOutput, calls=%fused_computation.194 | convolution fusion | flops 3307198976 | bytes 13842688 | tf_op jit(solution)/shard_map/dot_general | solution.py:188
  127.6 2.5 fusion.44
  131.4 17.9 %multiply_reduce_fusion = (f32[4,784]{1,0:T(4,128)S(1)}, f32[4,784,1568]{2,1,0:T(8,128)}) fusion(f32[4,784,1568]{2,1,0:T(8,128)} %get-tuple-element.45, f32[4,784]{1,0:T(4,128)S(1)} %get-tuple-element.44, bf16[784,4,64]{0,2,1:T(8,128)(2,1)} %bitcast.198, bf16[1568,4,64]{0,2,1:T(8,128)(2,1)} %bitcast.196), kind=kOutput, calls=%fused_computation.3 | convolution fusion | flops 644156352 | bytes 40567296 | tf_op jit(solution)/shard_map/gqhd,gkhd->ghqk/dot_general | solution.py:200
  149.3 13.8 %multiply_convert_fusion = bf16[4,784,1568]{2,1,0:T(8,128)(2,1)S(1)} fusion(f32[4,784,1568]{2,1,0:T(8,128)} %get-tuple-element.50, f32[4,784]{1,0:T(4,128)S(1)} %get-tuple-element.49, f32[4,784,1568]{2,1,0:T(8,128)} %get-tuple-element.45, f32[4,784]{1,0:T(4,128)S(1)} %get-tuple-element.44), kind=kLoop, calls=%fused_computation.2 | loop fusion | flops 19668992 | bytes 49197568 | tf_op jit(solution)/shard_map/convert_element_type | solution.py:204
  163.2 3.3 convolution_convert_fusion
  167.3 4.9 copy.132
  172.3 2.6 copy.180
  174.9 9.5 %fusion.16 = bf16[4,64,1568]{2,1,0:T(8,128)(2,1)} fusion(bf16[784,4,64]{0,2,1:T(8,128)(2,1)S(1)} %bitcast.199, f32[4,784]{1,0:T(4,128)S(1)} %get-tuple-element.44, bf16[784,4,64]{0,2,1:T(8,128)(2,1)S(1)} %bitcast.191, bf16[1568,4,64]{0,2,1:T(8,128)(2,1)} %bitcast.181), kind=kOutput, calls=%fused_computation.22 | convolution fusion | flops 1273973248 | bytes 2420992 | tf_op jit(solution)/shard_map/ghqk,gqhd->gkhd/dot_general | solution.py:211
  184.5 5.0 copy.134
  189.4 2.5 copy.179
  192.2 8.2 %fusion.58 = bf16[4,64,784]{2,1,0:T(8,128)(2,1)} fusion(bf16[1568,4,64]{0,2,1:T(8,128)(2,1)} %bitcast.182, bf16[4,784,1568]{2,1,0:T(8,128)(2,1)} %copy-done.2), kind=kOutput, calls=%fused_computation.77 | convolution fusion | flops 629809152 | bytes 11038720 | tf_op jit(solution)/shard_map/ghqk,gkhd->gqhd/dot_general | solution.py:205
  200.4 2.3 reshape_bitcast_fusion.1
  202.7 2.4 copy.133
  205.2 2.3 reshape_bitcast_fusion
  207.5 2.4 copy.135
  209.9 2.8 fusion.143
  214.3 25.0 %all-reduce.9.cloned.1.call-done = bf16[157,512]{1,0:T(8,128)(2,1)} async-done(((bf16[157,512]{1,0:T(8,128)(2,1)}), bf16[157,512]{1,0:T(8,128)(2,1)}) %all-reduce.9.cloned.1.call-update) | async-done | bytes 160784 | tf_op jit(solution)/shard_map/psum | solution.py:233
  248.2 4.8 fusion.19
  255.0 7.8 %fusion.84 = f32[1408,3,704]{2,0,1:T(8,128)} fusion(bf16[3,704,157]{1,0,2:T(4,128)(2,1)} %dot_general.125, f32[1408]{0:T(1024)S(1)} %copy-done.21, bf16[1,157,1408]{2,1,0:T(8,128)(2,1)S(1)} %copy-done.4, f32[157]{0:T(256)S(1)} %copy-done.23, f32[157]{0:T(256)S(1)} %copy-done.25), kind=kOutput, calls=%fused_computation.118 | convolution fusion | flops 934845824 | bytes 13006952 | tf_op jit(solution)/shard_map/dot_general | solution.py:268
  263.8 2.9 fusion.115
  266.7 203.5 %fusion = f32[704,24]{0,1:T(8,128)S(1)} fusion(f32[704,1408]{0,1:T(8,128)} %fusion.115), kind=kCustom, calls=%all-reduce-scatter | all-reduce-scatter fusion | flops 1081345 | bytes 4033024
  472.1 3.3 collective-permute-start
  475.5 10.1 %collective-permute-start.1 = (f32[704,24]{0,1:T(8,128)S(1)}, f32[704,24]{0,1:T(8,128)S(1)}, u32[]{:S(2)}, u32[]{:S(2)}) collective-permute-start(f32[704,24]{0,1:T(8,128)S(1)} %fusion), channel_id=1, source_target_pairs={{0,4},{2,6},{4,8},{6,10},{8,12},{10,14},{12,16},{14,18},{16,20},{1... | collective-permute-start | bytes 202760
  485.5 12.3 %collective-permute-start.2 = (f32[704,24]{0,1:T(8,128)S(1)}, f32[704,24]{0,1:T(8,128)S(1)}, u32[]{:S(2)}, u32[]{:S(2)}) collective-permute-start(f32[704,24]{0,1:T(8,128)S(1)} %fusion), channel_id=1, source_target_pairs={{0,6},{2,8},{4,10},{6,12},{8,14},{10,16},{12,18},{14,20},{16,22},{... | collective-permute-start | bytes 202760
  497.9 9.4 %collective-permute-start.3 = (f32[704,24]{0,1:T(8,128)S(1)}, f32[704,24]{0,1:T(8,128)S(1)}, u32[]{:S(2)}, u32[]{:S(2)}) collective-permute-start(f32[704,24]{0,1:T(8,128)S(1)} %fusion), channel_id=1, source_target_pairs={{0,8},{2,10},{4,12},{6,14},{8,16},{10,18},{12,20},{14,22},{16,24},... | collective-permute-start | bytes 202760
  511.2 6.9 %collective-permute-done.4 = f32[704,24]{0,1:T(8,128)S(1)} collective-permute-done((f32[704,24]{0,1:T(8,128)S(1)}, f32[704,24]{0,1:T(8,128)S(1)}, u32[]{:S(2)}, u32[]{:S(2)}) %collective-permute-start.4) | collective-permute-done | bytes 67616
  (169 shorter events, 51.6 us)
Async XLA Ops:
  7.2 106.2 %copy-start = (bf16[512,2048]{1,0:T(8,128)(2,1)S(1)}, bf16[512,2048]{1,0:T(8,128)(2,1)}, u32[]{:S(2)}) copy-start(bf16[512,2048]{1,0:T(8,128)(2,1)} %param.27) | copy-start | bytes 6291460
  7.2 51.0 %reduce-scatter.13.cloned.1.call-start = ((), (), s32[]{:S(2)}) async-start(), calls=%async_computation.5 | async-start | bytes 2162688
  12.7 4.0 copy-start.30
  16.2 6.4 %copy-start.3 = (bf16[1,157,1408]{2,1,0:T(8,128)(2,1)}, bf16[1,157,1408]{2,1,0:T(8,128)(2,1)S(1)}, u32[]{:S(2)}) copy-start(bf16[1,157,1408]{2,1,0:T(8,128)(2,1)S(1)} %copy.105) | copy-start | bytes 1326340
  16.3 6.2 %copy-start.24 = (f32[157]{0:T(256)}, f32[157]{0:T(256)S(1)}, u32[]{:S(2)}) copy-start(f32[157]{0:T(256)S(1)} %broadcast_multiply_fusion.8) | copy-start | bytes 1888
  16.6 5.9 %copy-start.22 = (f32[157]{0:T(256)}, f32[157]{0:T(256)S(1)}, u32[]{:S(2)}) copy-start(f32[157]{0:T(256)S(1)} %add_rsqrt_fusion.2) | copy-start | bytes 1888
  16.7 5.9 %copy-start.20 = (f32[1408]{0:T(1024)}, f32[1408]{0:T(1024)S(1)}, u32[]{:S(2)}) copy-start(f32[1408]{0:T(1024)S(1)} %convert_element_type.203) | copy-start | bytes 16900
  23.1 4.2 copy-start.10
  24.6 4.4 copy-start.12
  25.7 1.6 copy-start.17
  27.3 1.8 copy-start.27
  29.5 0.7 copy-start.8
  37.0 1.5 copy-start.29
  38.2 162.1 %reduce-scatter.15.cloned.1.call-start = ((), (), s32[]{:S(2)}) async-start(), calls=%async_computation.6 | async-start | bytes 1204224
  52.2 2.7 copy-start.33
  52.2 5.2 copy-start.26
  54.9 8.6 %copy-start.6 = (bf16[1408,512]{1,0:T(8,128)(2,1)S(1)}, bf16[1408,512]{1,0:T(8,128)(2,1)}, u32[]{:S(2)}) copy-start(bf16[1408,512]{1,0:T(8,128)(2,1)} %param.21) | copy-start | bytes 4325380
  70.7 2.5 copy-start.15
  110.9 2.5 copy-start.31
  112.5 0.9 copy-start.7
  127.6 2.5 copy-start.19
  163.2 4.2 copy-start.2
  172.3 2.6 copy-start.16
  174.8 30.3 %reduce-scatter.17.cloned.1.call-start = ((), (), s32[]{:S(2)}) async-start(), calls=%async_computation.7 | async-start | bytes 1204224
  191.9 47.4 %all-reduce.9.cloned.1.call-start = ((), (), s32[]{:S(2)}) async-start(), calls=%async_computation.3 | async-start | bytes 327680 | tf_op jit(solution)/shard_map/psum | solution.py:233
  214.2 27.2 %copy-start.5 = (bf16[704,1408]{1,0:T(8,128)(2,1)S(1)}, bf16[704,1408]{1,0:T(8,128)(2,1)}, u32[]{:S(2)}) copy-start(bf16[704,1408]{1,0:T(8,128)(2,1)} %param.20) | copy-start | bytes 5947396
  214.3 305.3 %all-reduce.11.cloned.1.call-start = ((), (), s32[]{:S(2)}) async-start(), calls=%async_computation.4 | async-start | bytes 901120 | tf_op jit(solution)/shard_map/psum | solution.py:263
  241.4 1.2 copy-start.28
  242.6 1.8 copy-start.14
  242.6 1.8 copy-start.18
  244.8 1.0 copy-start.13
  244.8 1.3 copy-start.11
  253.0 2.0 copy-start.4
  253.0 2.0 copy-start.21
  253.0 2.0 copy-start.23
  253.0 2.0 copy-start.25
  254.6 268.1 %all-reduce.13.cloned.1.call-start = ((), (), s32[]{:S(2)}) async-start(), calls=%async_computation.8 | async-start | bytes 25952256
  262.8 0.9 copy-start.9
  266.7 242.6 %copy-start.32 = (u32[128]{0:T(128)S(1)}, u32[128]{0:T(128)}, u32[]{:S(2)}) copy-start(u32[128]{0:T(128)} %constant.68) | copy-start | bytes 1540
  470.2 37.1 %collective-permute-start.5 = (f32[704,6]{0,1:T(8,128)S(1)}, f32[704,6]{0,1:T(8,128)S(1)}, u32[]{:S(2)}, u32[]{:S(2)}) collective-permute-start(f32[704,6]{0,1:T(8,128)S(1)} %slice.49), channel_id=1, source_target_pairs={{0,12},{2,14},{4,16},{6,18},{8,20},{10,22},{12,24},{14,26},{16,28}... | collective-permute-start | bytes 50696
  472.1 39.0 %collective-permute-start = (f32[704,24]{0,1:T(8,128)S(1)}, f32[704,24]{0,1:T(8,128)S(1)}, u32[]{:S(2)}, u32[]{:S(2)}) collective-permute-start(f32[704,24]{0,1:T(8,128)S(1)} %fusion), channel_id=1, source_target_pairs={{0,2},{2,4},{4,6},{6,8},{8,10},{10,12},{12,14},{14,16},{16,18},{18... | collective-permute-start | bytes 202760
  475.5 35.7 %collective-permute-start.1 = (f32[704,24]{0,1:T(8,128)S(1)}, f32[704,24]{0,1:T(8,128)S(1)}, u32[]{:S(2)}, u32[]{:S(2)}) collective-permute-start(f32[704,24]{0,1:T(8,128)S(1)} %fusion), channel_id=1, source_target_pairs={{0,4},{2,6},{4,8},{6,10},{8,12},{10,14},{12,16},{14,18},{16,20},{1... | collective-permute-start | bytes 202760
  485.5 25.6 %collective-permute-start.2 = (f32[704,24]{0,1:T(8,128)S(1)}, f32[704,24]{0,1:T(8,128)S(1)}, u32[]{:S(2)}, u32[]{:S(2)}) collective-permute-start(f32[704,24]{0,1:T(8,128)S(1)} %fusion), channel_id=1, source_target_pairs={{0,6},{2,8},{4,10},{6,12},{8,14},{10,16},{12,18},{14,20},{16,22},{... | collective-permute-start | bytes 202760
  497.9 13.3 %collective-permute-start.3 = (f32[704,24]{0,1:T(8,128)S(1)}, f32[704,24]{0,1:T(8,128)S(1)}, u32[]{:S(2)}, u32[]{:S(2)}) collective-permute-start(f32[704,24]{0,1:T(8,128)S(1)} %fusion), channel_id=1, source_target_pairs={{0,8},{2,10},{4,12},{6,14},{8,16},{10,18},{12,20},{14,22},{16,24},... | collective-permute-start | bytes 202760
  507.3 10.8 %collective-permute-start.4 = (f32[704,24]{0,1:T(8,128)S(1)}, f32[704,24]{0,1:T(8,128)S(1)}, u32[]{:S(2)}, u32[]{:S(2)}) collective-permute-start(f32[704,24]{0,1:T(8,128)S(1)} %fusion), channel_id=1, source_target_pairs={{0,10},{2,12},{4,14},{6,16},{8,18},{10,20},{12,22},{14,24},{16,26}... | collective-permute-start | bytes 202760
  520.9 3.5 copy-start.1
Sparse Core Ops, SparseCore 0:
  38.4 13.0 reduce-scatter.12
  175.0 12.3 reduce-scatter.14
  192.0 12.3 reduce-scatter.16
  214.4 24.9 all-reduce.8
  254.8 25.4 all-reduce.10
  285.6 210.7 all-reduce.12
where the time goes:
time: 538 us; the launch traced here: 532 us
  blocking collectives  218 us (41%)
  matrix products  120 us (22%)
  local copies, waits for them, and re-layouts  73.3 us (14%)
  starting transfers between devices  39.9 us (7%)
  waiting for transfers between devices  32.1 us (6%)
  other arithmetic  31.9 us (6%)
  between operations  16.7 us (3%)
    unnamed x1, blocking collectives  204 us
    unnamed x88, local copies, waits for them, and re-layouts  46.1 us
    unnamed x10, starting transfers between devices  39.6 us
    psum x1, waiting for transfers between devices, per_device(): grad_lowered = lax.psum(back_rows.astype(jnp.bfloat16), 'fsdp')  25 us
    dot_general x1, matrix products, per_device(): jnp.einsum('gqhd,gkhd->ghqk', grad_mix, values_heads, preferred_element_t...  17.9 us
    convert_element_type x1, other arithmetic, per_device(): grad_scores = (dec_probs * (grad_probs - centre)).astype(jnp.bfloat16)  13.8 us
    sub x1, matrix products, per_device(): shifted = jnp.exp(dec_scores - row_max)  11.2 us
  transfers between devices with their start and end apart: 12, of which 2 were waited for; matrix products, arithmetic and copies ran while one was open for 51% of the time, Pallas kernels for 0%

commit v1 on v0

v1 whole, which is shorter than its diff:
```python
import functools
import math

import jax
import jax.numpy as jnp
import numpy as np
from jax import lax
from jax.experimental import pallas as pl
from jax.experimental.pallas import tpu as pltpu
from jax.sharding import PartitionSpec as P

D = 1408
HALF = 704
HD = 88
HEADS = 8
DD = 512
DHD = 64
DH = 4
DI = 256
DF = 2048
TUBES = 1568
VIS = 157
ROWS = 160
OWN = 784
BLK = 112
EPS = 1e-06
ENC_SCALE = HD ** (-0.5)
DEC_SCALE = DHD ** (-0.5)
SQRT_HALF = 0.7071067811865476
INV_SQRT_TWO_PI = 0.3989422804014327
F32 = jnp.float32
BF16 = jnp.bfloat16
MESH = pl.DeviceIdType.MESH


def nn(a, b):
    return lax.dot_general(a, b, (((1,), (0,)), ((), ())), preferred_element_type=F32)


def nt(a, b):
    return lax.dot_general(a, b, (((1,), (1,)), ((), ())), preferred_element_type=F32)


def tn(a, b):
    return lax.dot_general(a, b, (((0,), (0,)), ((), ())), preferred_element_type=F32)


def norm_parts(values, width):
    mean = jnp.sum(values, axis=-1, keepdims=True) * (1.0 / width)
    centred = values - mean
    inv = lax.rsqrt(jnp.sum(centred * centred, axis=-1, keepdims=True) * (1.0 / width) + EPS)
    return centred * inv, inv


def norm_back(grad, normed, inv, gain, width):
    scaled = grad * gain
    first = jnp.sum(scaled, axis=-1, keepdims=True) * (1.0 / width)
    second = jnp.sum(scaled * normed, axis=-1, keepdims=True) * (1.0 / width)
    return inv * (scaled - first - normed * second)


def gelu_slope(u):
    e = jnp.exp(u * u * -0.5)
    t = 1.0 / (1.0 + (0.3275911 * SQRT_HALF) * jnp.abs(u))
    poly = t * (0.254829592 + t * (-0.284496736 + t * (1.421413741 + t * (-1.453152027 + t * 1.061405429))))
    tail = (0.5 * e) * poly
    return jnp.where(u >= 0.0, 1.0 - tail, tail) + u * e * INV_SQRT_TWO_PI


def position_rows():
    rates = np.exp(np.arange(DD // 2, dtype=np.float32) * np.float32(-2.0 * math.log(10000.0) / DD))
    angles = np.arange(TUBES, dtype=np.float32)[:, None] * rates
    return np.stack([np.sin(angles), np.cos(angles)], axis=-1).reshape(TUBES, DD).astype(np.float32)


def main_kernel(
    tok, visr, visc, rank, genc, maskt, gain1, gain2,
    wt_h, proj_h, down_h, dqkv_h, dproj_h, fc1_h, fc2_h, cot_h, pos_h,
    gtok, hid_o, gqkv_o, mixed_o, gel_o,
    wt, proj, down, dqkv, dproj, fc1, fc2, cot, pos,
    tokpad, tokrecv, xfull, invs, qs, ks, vs, lows, lowr,
    xall, kd, vd, xown, qd, mixd, mxs, lis, mlp, acc, gmid, gmix, cen,
    exs, exr, hts, htr, sts, strr,
    local, send, recv,
):
    me = lax.axis_index("fsdp")
    other = 1 - me
    first = me == 0

    loads = [
        pltpu.make_async_copy(src, dst, local.at[i])
        for i, (src, dst) in enumerate(
            [(wt_h, wt), (pos_h, pos), (proj_h, proj), (down_h, down), (dqkv_h, dqkv),
             (dproj_h, dproj), (fc1_h, fc1), (fc2_h, fc2), (cot_h, cot)]
        )
    ]
    for load in loads:
        load.start()
    l_wt, l_pos, l_proj, l_down, l_dqkv, l_dproj, l_fc1, l_fc2, l_cot = loads

    def exchange(src, dst, i):
        return pltpu.make_async_remote_copy(
            src_ref=src, dst_ref=dst, send_sem=send.at[i], recv_sem=recv.at[i],
            device_id={"fsdp": other}, device_id_type=MESH,
        )

    barrier = pltpu.get_barrier_semaphore()
    pl.semaphore_signal(barrier, inc=1, device_id={"fsdp": other}, device_id_type=MESH)

    tokpad[...] = jnp.zeros((ROWS, HALF), BF16)
    tokpad[0:VIS, :] = tok[...]
    pl.semaphore_wait(barrier, 1)
    swap = exchange(tokpad, tokrecv, 0)
    swap.start()

    vis_row = visr[...]
    vis_col = visc[...]
    lane_tube = lax.broadcasted_iota(jnp.int32, (ROWS, TUBES), 1)
    vis_hit = lane_tube == vis_col
    vis_pick = vis_hit.astype(F32).astype(BF16)
    slot_of = jnp.sum(jnp.where(vis_hit, rank[...] + 1, 0), axis=1, keepdims=True) - 1
    own_pick = (lax.broadcasted_iota(jnp.int32, (ROWS, OWN), 1) == slot_of).astype(F32).astype(BF16)

    swap.wait()
    mine = tokpad[...].astype(F32)
    theirs = tokrecv[...].astype(F32)
    xfull[:, 0:HALF] = jnp.where(first, mine, theirs)
    xfull[:, HALF:D] = jnp.where(first, theirs, mine)
    values = xfull[...]
    normed, inv = norm_parts(values, D)
    invs[...] = inv
    gain_enc = genc[...].astype(F32)
    hidden = (normed * gain_enc).astype(BF16)
    hid_o[...] = hidden
    l_wt.wait()
    qs[...] = (nt(hidden, wt[0:HALF, :]) * ENC_SCALE).astype(BF16)
    ks[...] = nt(hidden, wt[HALF:2 * HALF, :]).astype(BF16)
    vs[...] = nt(hidden, wt[2 * HALF:3 * HALF, :]).astype(BF16)
    key_ok = lax.broadcasted_iota(jnp.int32, (ROWS, ROWS), 1) < VIS

    def enc_probs(h):
        lanes = slice(h * HD, (h + 1) * HD)
        s = nt(qs[:, lanes], ks[:, lanes])
        s = jnp.where(key_ok, s, -1e30)
        e = jnp.exp(s - jnp.max(s, axis=-1, keepdims=True))
        return e / jnp.sum(e, axis=-1, keepdims=True)

    for h in range(HEADS):
        lanes = slice(h * HD, (h + 1) * HD)
        mixed_o[:, lanes] = nn(enc_probs(h).astype(BF16), vs[:, lanes]).astype(BF16)
    l_proj.wait()
    heads_term = nn(mixed_o[...], proj[...])
    part_enc = (jnp.where(first, xfull[...], 0.0) + heads_term).astype(BF16)
    l_down.wait()
    lows[...] = nn(part_enc, down[...])
    swap = exchange(lows, lowr, 1)
    swap.start()

    swap.wait()
    lowered = (lows[...] + lowr[...]).astype(BF16)
    l_pos.wait()
    l_dqkv.wait()
    gain_one = gain1[...].astype(F32)
    gain_two = gain2[...].astype(F32)
    mask_row = maskt[...].astype(F32)

    @pl.loop(0, TUBES // BLK)
    def _(b):
        rows = pl.ds(pl.multiple_of(b * BLK, BLK), BLK)
        hit = lax.broadcasted_iota(jnp.int32, (BLK, ROWS), 0) + b * BLK == vis_row
        hit = hit.astype(F32)
        placed = nn(hit.astype(BF16), lowered)
        covered = jnp.sum(hit, axis=1, keepdims=True)
        start = (placed + (1.0 - covered) * mask_row + pos[rows, :]).astype(BF16)
        xall[rows, :] = start
        n1, _ = norm_parts(start.astype(F32), DD)
        attn_in = (n1 * gain_one).astype(BF16)
        kv = nn(attn_in, dqkv[:, DI:3 * DI]).astype(BF16)
        for h in range(DH):
            kd[h, rows, :] = kv[:, h * DHD:(h + 1) * DHD]
            vd[h, rows, :] = kv[:, DI + h * DHD:DI + (h + 1) * DHD]

    @pl.loop(0, OWN // BLK)
    def _(b):
        rows = pl.ds(pl.multiple_of(b * BLK, BLK), BLK)
        pick = lax.broadcasted_iota(jnp.int32, (BLK, TUBES), 0) + b * BLK == rank[...]
        start = nn(pick.astype(F32).astype(BF16), xall[...])
        xown[rows, :] = start
        n1, _ = norm_parts(start, DD)
        attn_in = (n1 * gain_one).astype(BF16)
        q = (nn(attn_in, dqkv[:, 0:DI]) * DEC_SCALE).astype(BF16)
        for h in range(DH):
            qd[h, rows, :] = q[:, h * DHD:(h + 1) * DHD]

    @pl.loop(0, OWN // BLK)
    def _(b):
        rows = pl.ds(pl.multiple_of(b * BLK, BLK), BLK)
        for h in range(DH):
            s = nt(qd[h, rows, :], kd[h])
            top = jnp.max(s, axis=-1, keepdims=True)
            e = jnp.exp(s - top)
            total = 1.0 / jnp.sum(e, axis=-1, keepdims=True)
            mxs[h, rows, :] = top
            lis[h, rows, :] = total
            mixd[rows, h * DHD:(h + 1) * DHD] = nn(e.astype(BF16), vd[h]) * total

    l_dproj.wait()

    def after(rows):
        return (xown[rows, :] + nn(mixd[rows, :].astype(BF16), dproj[...])).astype(BF16).astype(F32)

    @pl.loop(0, OWN // BLK)
    def _(b):
        rows = pl.ds(pl.multiple_of(b * BLK, BLK), BLK)
        n2, _ = norm_parts(after(rows), DD)
        mlp[rows, :] = (n2 * gain_two).astype(BF16)

    l_fc1.wait()
    l_fc2.wait()
    l_cot.wait()
    acc[...] = jnp.zeros((OWN, DD), F32)

    @pl.loop(0, DF // 256)
    def _(c):
        part = pl.ds(pl.multiple_of(c * 256, 256), 256)
        up = nn(mlp[...], fc1[:, part])
        gact = nt(cot[...], fc2[part, :])
        gup = (gact * gelu_slope(up)).astype(BF16)
        acc[...] += nt(gup, fc1[:, part])

    @pl.loop(0, OWN // BLK)
    def _(b):
        rows = pl.ds(pl.multiple_of(b * BLK, BLK), BLK)
        n2, inv2 = norm_parts(after(rows), DD)
        g = cot[rows, :].astype(F32) + norm_back(acc[rows, :], n2, inv2, gain_two, DD)
        low = g.astype(BF16)
        gmid[rows, :] = low
        gm = nt(low, dproj[...]).astype(BF16)
        prod = gm.astype(F32) * mixd[rows, :]
        for h in range(DH):
            lanes = slice(h * DHD, (h + 1) * DHD)
            gmix[h, rows, :] = gm[:, lanes]
            cen[h, rows, :] = jnp.sum(prod[:, lanes], axis=-1, keepdims=True)

    vis_x = nn(vis_pick, xall[...])
    exs[:, 3 * DI:] = nn(own_pick, gmid[...]).astype(BF16)
    for h in range(DH):
        lanes = slice(h * DHD, (h + 1) * DHD)
        k_vis = nn(vis_pick, kd[h]).astype(BF16)
        v_vis = nn(vis_pick, vd[h]).astype(BF16)
        p = jnp.exp(nt(qd[h], k_vis) - mxs[h]) * lis[h]
        ds = (p * (nt(gmix[h], v_vis) - cen[h])).astype(BF16)
        exs[:, DI + h * DHD:DI + (h + 1) * DHD] = tn(ds, qd[h]).astype(BF16)
        exs[:, 2 * DI + h * DHD:2 * DI + (h + 1) * DHD] = tn(p.astype(BF16), gmix[h]).astype(BF16)
        q_vis = nn(own_pick, qd[h]).astype(BF16)
        g_vis = nn(own_pick, gmix[h]).astype(BF16)
        s = nt(q_vis, kd[h])
        e = jnp.exp(s - jnp.max(s, axis=-1, keepdims=True))
        p = e * (1.0 / jnp.sum(e, axis=-1, keepdims=True))
        g = nt(g_vis, vd[h])
        c = jnp.sum(p * g, axis=-1, keepdims=True)
        ds = (p * (g - c)).astype(BF16)
        exs[:, lanes] = (nn(ds, kd[h]) * DEC_SCALE).astype(BF16)

    swap = exchange(exs, exr, 2)
    swap.start()
    swap.wait()
    both = exs[...].astype(F32) + exr[...].astype(F32)
    gattn = nt(both[:, 0:3 * DI].astype(BF16), dqkv[...])
    n1, inv1 = norm_parts(vis_x, DD)
    gstart = both[:, 3 * DI:] + norm_back(gattn, n1, inv1, gain_one, DD)
    real = lax.broadcasted_iota(jnp.int32, (ROWS, DD), 0) < VIS
    glow = jnp.where(real, gstart, 0.0).astype(BF16)

    genc_rows = nt(glow, down[...])
    gel = genc_rows.astype(BF16)
    gel_o[...] = gel
    xfull[...] = genc_rows
    gmx = nt(gel, proj[...]).astype(BF16)
    for h in range(HEADS):
        lanes = slice(h * HD, (h + 1) * HD)
        p = enc_probs(h)
        gm = gmx[:, lanes]
        g = nt(gm, vs[:, lanes])
        c = jnp.sum(p * g, axis=-1, keepdims=True)
        ds = (p * (g - c)).astype(BF16)
        gqkv_o[:, h * HD:(h + 1) * HD] = (nn(ds, ks[:, lanes]) * ENC_SCALE).astype(BF16)
        gqkv_o[:, HALF + h * HD:HALF + (h + 1) * HD] = tn(ds, qs[:, lanes]).astype(BF16)
        gqkv_o[:, 2 * HALF + h * HD:2 * HALF + (h + 1) * HD] = tn(p.astype(BF16), gm).astype(BF16)
    terms = nn(gqkv_o[...], wt[...]).astype(BF16)
    scaled = terms.astype(F32) * gain_enc
    mine = tokpad[...].astype(F32)
    theirs = tokrecv[...].astype(F32)
    full = jnp.concatenate([jnp.where(first, mine, theirs), jnp.where(first, theirs, mine)], axis=1)
    normed, inv = norm_parts(full, D)
    s1 = jnp.sum(scaled, axis=-1, keepdims=True)
    s2 = jnp.sum(scaled * normed, axis=-1, keepdims=True)
    sts[...] = jnp.where(lax.broadcasted_iota(jnp.int32, (ROWS, 128), 1) == 0, s1, s2)
    hts[...] = jnp.where(first, terms[:, HALF:], terms[:, 0:HALF])
    swap_a = exchange(hts, htr, 3)
    swap_b = exchange(sts, strr, 4)
    swap_a.start()
    swap_b.start()
    swap_a.wait()
    swap_b.wait()
    stats = sts[...] + strr[...]
    m1 = stats[:, 0:1] * (1.0 / D)
    m2 = stats[:, 1:2] * (1.0 / D)
    gh = jnp.where(first, terms[:, 0:HALF], terms[:, HALF:]).astype(F32) + htr[...].astype(F32)
    gain_mine = jnp.where(first, gain_enc[:, 0:HALF], gain_enc[:, HALF:])
    normed_mine = jnp.where(first, normed[:, 0:HALF], normed[:, HALF:])
    base = jnp.where(first, xfull[:, 0:HALF], xfull[:, HALF:D])
    out = base + inv * (gh * gain_mine - m1 - normed_mine * m2)
    gtok[...] = out[0:VIS, :]


def run_main(tok, visr, visc, rank, genc, maskt, gain1, gain2, wt, proj, down, dqkv, dproj, fc1, fc2, cot, pos):
    vm = pl.BlockSpec(memory_space=pltpu.VMEM)
    hbm = pl.BlockSpec(memory_space=pl.ANY)
    V = pltpu.VMEM
    big = (wt, proj, down, dqkv, dproj, fc1, fc2, cot, pos)
    scratch = [V(a.shape, a.dtype) for a in big] + [
        V((ROWS, HALF), BF16), V((ROWS, HALF), BF16), V((ROWS, D), F32), V((ROWS, 1), F32),
        V((ROWS, HALF), BF16), V((ROWS, HALF), BF16), V((ROWS, HALF), BF16),
        V((ROWS, DD), F32), V((ROWS, DD), F32),
        V((TUBES, DD), BF16), V((DH, TUBES, DHD), BF16), V((DH, TUBES, DHD), BF16),
        V((OWN, DD), F32), V((DH, OWN, DHD), BF16), V((OWN, DI), F32),
        V((DH, OWN, 1), F32), V((DH, OWN, 1), F32),
        V((OWN, DD), BF16), V((OWN, DD), F32), V((OWN, DD), BF16),
        V((DH, OWN, DHD), BF16), V((DH, OWN, 1), F32),
        V((ROWS, 3 * DI + DD), BF16), V((ROWS, 3 * DI + DD), BF16),
        V((ROWS, HALF), BF16), V((ROWS, HALF), BF16), V((ROWS, 128), F32), V((ROWS, 128), F32),
        pltpu.SemaphoreType.DMA((9,)), pltpu.SemaphoreType.DMA((5,)), pltpu.SemaphoreType.DMA((5,)),
    ]
    return pl.pallas_call(
        main_kernel,
        out_shape=(
            jax.ShapeDtypeStruct((VIS, HALF), F32),
            jax.ShapeDtypeStruct((ROWS, D), BF16),
            jax.ShapeDtypeStruct((ROWS, 3 * HALF), BF16),
            jax.ShapeDtypeStruct((ROWS, HALF), BF16),
            jax.ShapeDtypeStruct((ROWS, D), BF16),
        ),
        in_specs=[vm] * 8 + [hbm] * 9,
        out_specs=[vm] * 5,
        scratch_shapes=scratch,
        compiler_params=pltpu.CompilerParams(
            collective_id=0, has_side_effects=True, vmem_limit_bytes=60 * 1024 * 1024
        ),
    )(tok, visr, visc, rank, genc, maskt, gain1, gain2, *big)


def per_device(
    tokens, vis_index, owner, enc_gain, enc_qkv, enc_proj, to_decoder, mask_token, dec_gain1,
    dec_qkv, dec_proj, dec_gain2, dec_fc1, dec_fc2, cotangent,
):
    me = lax.axis_index("fsdp")
    mine = (owner == me).astype(jnp.int32)
    rank = jnp.where(mine == 1, jnp.cumsum(mine, axis=1) - 1, -1)
    vis = jnp.pad(vis_index, ((0, 0), (0, ROWS - VIS)), constant_values=-1)
    wt = jnp.transpose(enc_qkv, (1, 2, 0)).reshape(3 * HALF, D)
    gtok, hidden, gqkv, mixed, gel = run_main(
        tokens[0], vis, vis.reshape(ROWS, 1), rank, enc_gain[None], mask_token[None],
        dec_gain1[None], dec_gain2[None], wt, enc_proj, to_decoder, dec_qkv, dec_proj,
        dec_fc1, dec_fc2, cotangent[0], jnp.asarray(position_rows()),
    )
    qkv_term = jnp.dot(hidden.T, gqkv, preferred_element_type=F32).reshape(D, 3, HALF)
    proj_term = jnp.dot(mixed.T, gel, preferred_element_type=F32)
    return (
        gtok[None],
        lax.psum_scatter(qkv_term, "dp", scatter_dimension=0, tiled=True),
        lax.psum_scatter(proj_term, "dp", scatter_dimension=1, tiled=True),
    )


def solution(mesh):
    return jax.shard_map(
        per_device,
        mesh=mesh,
        in_specs=(
            P("dp", None, "fsdp"),
            P("dp", None),
            P("dp", None),
            P(),
            P(None, None, "fsdp"),
            P("fsdp", None),
            P(),
            P(),
            P(),
            P(),
            P(),
            P(),
            P(),
            P(),
            P("dp", "fsdp", None),
        ),
        out_specs=(P("dp", None, "fsdp"), P("dp", None, "fsdp"), P("fsdp", "dp")),
        check_vma=False,
    )
```

time: 538 us -> 380 us (0.71); the launches traced: 532 us -> 379 us
  matrix products: 120 us -> 10.3 us
  Pallas kernels: 0 us -> 79.8 us
  local copies, waits for them, and re-layouts: 73.3 us -> 27.3 us
  other arithmetic: 31.9 us -> 2.48 us
  waiting for transfers between devices: 32.1 us -> 5.35 us
  starting transfers between devices: 39.9 us -> 30.1 us
  blocking collectives: 218 us -> 209 us
    dot_general x26 -> x2, matrix products: 107 us -> 10.3 us  [the longest x1 7.44 us: per_device(): jnp.dot(hidden.T, gqkv, preferred_element_type=F32).reshape(D, 3, HALF)]
    pallas_call x0 -> x1, Pallas kernels: none -> 79.8 us  [run_main(): pl.pallas_call(main_kernel, out_shape=(jax.ShapeDtypeStruct((VIS, HALF),...]
    unnamed x88 -> x15, local copies, waits for them, and re-layouts: 46.1 us -> 6.27 us
    psum x2 -> x0, waiting for transfers between devices: 25 us -> none  [the longest x1 25 us: per_device(): grad_lowered = lax.psum(back_rows.astype(jnp.bfloat16), 'fsdp')]
    convert_element_type x9 -> x1, other arithmetic: 19.8 us -> 0.7 us  [per_device(): mine = (owner == me).astype(jnp.int32)]
    sub x2 -> x0, matrix products: 12.7 us -> none  [the longest x1 11.2 us: per_device(): shifted = jnp.exp(dec_scores - row_max)]
    all_gather x3 -> x0, blocking collectives: 9.77 us -> none  [the longest x1 4.3 us: per_device(): value_piece = lax.all_gather(dec_values, 'fsdp', axis=1, tiled=True)]
    unnamed x10 -> x7, starting transfers between devices: 39.6 us -> 30.1 us
  transfers between devices with their start and end apart: 12 -> 7, of which waited for: 2 -> 2; matrix products, arithmetic and copies ran while one was open for 51% -> 57% of each run, Pallas kernels for 0% -> 0%
where the time goes in v1:
time: 380 us; the launch traced here: 379 us
  blocking collectives  209 us (55%)
  Pallas kernels  79.8 us (21%)
  starting transfers between devices  30.1 us (8%)
  local copies, waits for them, and re-layouts  27.3 us (7%)
  between operations  15.5 us (4%)
  matrix products  10.3 us (3%)
  waiting for transfers between devices  5.35 us (1%)
    unnamed x1, blocking collectives  209 us
    pallas_call x1, Pallas kernels, run_main(): pl.pallas_call(main_kernel, out_shape=(jax.ShapeDtypeStruct((VIS, HALF),...  79.8 us
    unnamed x7, starting transfers between devices  30.1 us
    reshape x1, local copies, waits for them, and re-layouts, per_device(): jnp.dot(hidden.T, gqkv, preferred_element_type=F32).reshape(D, 3, HALF)  13.7 us
  transfers between devices with their start and end apart: 7, of which 2 were waited for; matrix products, arithmetic and copies ran while one was open for 57% of the time, Pallas kernels for 0%

profile of v1, /device:TPU:96, one launch (start us, length us, event | category | flops | bytes accessed | tf_op | source)
XLA Modules:
  0.0 379.4 jit_solution(7219786061361220083)
XLA Ops:
  7.2 0.0 all-reduce.7.cloned.1.call-start
  7.2 1.3 broadcast_in_dim.18.maskt
  8.5 1.3 broadcast_in_dim.19.gain1
  9.8 1.3 broadcast_in_dim.20.gain2
  11.0 1.3 pad_bitcast_fusion
  12.3 1.3 broadcast_in_dim.17.genc
  13.6 0.7 compare_convert_fusion
  14.3 0.3 reduce-window.6
  14.6 0.2 slice_reduce_fusion
  14.8 0.2 reduce-window.9
  15.0 0.1 broadcast_bitcast_fusion
  15.0 0.8 copy.24.visc
  15.8 1.3 compare_select_fusion.rank
  17.1 79.8 %shard_map.175 = (f32[157,704]{1,0:T(8,128)}, bf16[160,1408]{1,0:T(8,128)(2,1)}, bf16[160,2112]{1,0:T(8,128)(2,1)}, bf16[160,704]{1,0:T(8,128)(2,1)}, bf16[160,1408]{1,0:T(8,128)(2,1)}) custom-call(bf16[157,704]{1,0:T(8,128)(2,1)} %bitcast.34, s32[1,160]{1,0:T(1,128)} %get-tuple-element.23.visr, s32[160,1]{1,0:T(8,128)} %copy.24.visc, ...), custom_call_target="tpu_custom_call" | custom-call | tf_op jit(solution)/shard_map/pallas_call | solution.py:335
  96.9 7.4 %fusion.3 = f32[1408,2112]{0,1:T(8,128)} fusion(bf16[160,1408]{1,0:T(8,128)(2,1)} %get-tuple-element.9, bf16[160,2112]{1,0:T(8,128)(2,1)} %get-tuple-element.10), kind=kOutput, calls=%fused_computation.14 | convolution fusion | flops 951582720 | bytes 13021184 | tf_op jit(solution)/shard_map/dot_general | solution.py:367
  104.3 13.7 %copy.25 = f32[1408,3,704]{2,0,1:T(8,128)} copy(f32[1408,3,704]{0,2,1:T(8,128)} %bitcast.30) | data formatting | bytes 23789568 | tf_op jit(solution)/shard_map/reshape | solution.py:367
  118.0 0.0 copy-start
  118.0 0.0 copy-start.2
  118.0 0.0 all-reduce.7.cloned.1.call-update
  118.0 0.9 copy-done
  119.0 0.2 copy-done.2
  119.2 0.0 copy-start.1
  119.2 2.9 fusion.4
  122.1 0.0 copy-start.3
  122.1 208.6 %fusion = f32[704,24]{0,1:T(8,128)S(1)} fusion(f32[704,1408]{0,1:T(8,128)} %fusion.4), kind=kCustom, calls=%all-reduce-scatter | all-reduce-scatter fusion | flops 1081345 | bytes 4033024
  330.6 1.9 collective-permute-start.5
  332.6 9.9 %collective-permute-start.4 = (f32[704,24]{0,1:T(8,128)S(1)}, f32[704,24]{0,1:T(8,128)S(1)}, u32[]{:S(2)}, u32[]{:S(2)}) collective-permute-start(f32[704,24]{0,1:T(8,128)S(1)} %fusion), channel_id=1, source_target_pairs={{0,10},{2,12},{4,14},{6,16},{8,18},{10,20},{12,22},{14,24},{16,26}... | collective-permute-start | bytes 202760
  342.5 10.4 %collective-permute-start.3 = (f32[704,24]{0,1:T(8,128)S(1)}, f32[704,24]{0,1:T(8,128)S(1)}, u32[]{:S(2)}, u32[]{:S(2)}) collective-permute-start(f32[704,24]{0,1:T(8,128)S(1)} %fusion), channel_id=1, source_target_pairs={{0,8},{2,10},{4,12},{6,14},{8,16},{10,18},{12,20},{14,22},{16,24},... | collective-permute-start | bytes 202760
  352.9 1.9 collective-permute-start.2
  354.9 4.0 %collective-permute-start.1 = (f32[704,24]{0,1:T(8,128)S(1)}, f32[704,24]{0,1:T(8,128)S(1)}, u32[]{:S(2)}, u32[]{:S(2)}) collective-permute-start(f32[704,24]{0,1:T(8,128)S(1)} %fusion), channel_id=1, source_target_pairs={{0,4},{2,6},{4,8},{6,10},{8,12},{10,14},{12,16},{14,18},{16,20},{1... | collective-permute-start | bytes 202760
  358.8 0.0 collective-permute-done.5
  358.9 1.9 collective-permute-start
  360.8 0.0 copy-done.1
  360.8 1.3 copy.26
  362.1 0.0 copy-done.3
  362.1 0.6 fusion.2
  364.0 0.0 collective-permute-done.4
  364.0 0.0 collective-permute-done.3
  364.0 0.0 collective-permute-done.2
  364.0 1.6 collective-permute-done.1
  365.6 3.7 collective-permute-done
  369.3 0.9 concatenate
  370.2 0.6 constant_dynamic-slice_fusion
  370.9 0.0 all-reduce.7.cloned.1.call-done
  370.9 1.7 constant_dynamic-slice_fusion.1
  (4 shorter events, 0.0 us)
Async XLA Ops:
  7.2 363.7 %all-reduce.7.cloned.1.call-start = ((), (), s32[]{:S(2)}) async-start(), calls=%async_computation | async-start | bytes 25952256
  118.0 0.9 copy-start
  118.0 1.1 copy-start.2
  119.2 241.6 %copy-start.1 = (f32[157,704]{1,0:T(8,128)S(1)}, f32[157,704]{1,0:T(8,128)}, u32[]{:S(2)}) copy-start(f32[157,704]{1,0:T(8,128)} %get-tuple-element.8) | copy-start | bytes 1326340
  122.1 240.0 %copy-start.3 = (u32[128]{0:T(128)S(1)}, u32[128]{0:T(128)}, u32[]{:S(2)}) copy-start(u32[128]{0:T(128)} %constant.26) | copy-start | bytes 1540
  330.6 28.2 %collective-permute-start.5 = (f32[704,6]{0,1:T(8,128)S(1)}, f32[704,6]{0,1:T(8,128)S(1)}, u32[]{:S(2)}, u32[]{:S(2)}) collective-permute-start(f32[704,6]{0,1:T(8,128)S(1)} %slice.15), channel_id=1, source_target_pairs={{0,12},{2,14},{4,16},{6,18},{8,20},{10,22},{12,24},{14,26},{16,28}... | collective-permute-start | bytes 50696
  332.6 31.4 %collective-permute-start.4 = (f32[704,24]{0,1:T(8,128)S(1)}, f32[704,24]{0,1:T(8,128)S(1)}, u32[]{:S(2)}, u32[]{:S(2)}) collective-permute-start(f32[704,24]{0,1:T(8,128)S(1)} %fusion), channel_id=1, source_target_pairs={{0,10},{2,12},{4,14},{6,16},{8,18},{10,20},{12,22},{14,24},{16,26}... | collective-permute-start | bytes 202760
  342.5 21.5 %collective-permute-start.3 = (f32[704,24]{0,1:T(8,128)S(1)}, f32[704,24]{0,1:T(8,128)S(1)}, u32[]{:S(2)}, u32[]{:S(2)}) collective-permute-start(f32[704,24]{0,1:T(8,128)S(1)} %fusion), channel_id=1, source_target_pairs={{0,8},{2,10},{4,12},{6,14},{8,16},{10,18},{12,20},{14,22},{16,24},... | collective-permute-start | bytes 202760
  352.9 11.1 %collective-permute-start.2 = (f32[704,24]{0,1:T(8,128)S(1)}, f32[704,24]{0,1:T(8,128)S(1)}, u32[]{:S(2)}, u32[]{:S(2)}) collective-permute-start(f32[704,24]{0,1:T(8,128)S(1)} %fusion), channel_id=1, source_target_pairs={{0,6},{2,8},{4,10},{6,12},{8,14},{10,16},{12,18},{14,20},{16,22},{... | collective-permute-start | bytes 202760
  354.9 10.8 %collective-permute-start.1 = (f32[704,24]{0,1:T(8,128)S(1)}, f32[704,24]{0,1:T(8,128)S(1)}, u32[]{:S(2)}, u32[]{:S(2)}) collective-permute-start(f32[704,24]{0,1:T(8,128)S(1)} %fusion), channel_id=1, source_target_pairs={{0,4},{2,6},{4,8},{6,10},{8,12},{10,14},{12,16},{14,18},{16,20},{1... | collective-permute-start | bytes 202760
  358.9 10.5 %collective-permute-start = (f32[704,24]{0,1:T(8,128)S(1)}, f32[704,24]{0,1:T(8,128)S(1)}, u32[]{:S(2)}, u32[]{:S(2)}) collective-permute-start(f32[704,24]{0,1:T(8,128)S(1)} %fusion), channel_id=1, source_target_pairs={{0,2},{2,4},{4,6},{6,8},{8,10},{10,12},{12,14},{14,16},{16,18},{18... | collective-permute-start | bytes 202760
Sparse Core Ops, SparseCore 0:
  118.2 214.6 all-reduce.6

commit v2 on v1

--- a/solution.py
+++ b/solution.py
@@ -350,6 +350,148 @@
     )(tok, visr, visc, rank, genc, maskt, gain1, gain2, *big)
 
 
+PADW = 1536
+QB = 528
+PB = 176
+TILE = 384
+
+
+def weight_kernel(hid, gel, rq, rp, oq, op, hidg, gelg, rqg, rpg, ca, cb, ra, rb, sa, sb, ta, tb, fa, fb, ga, gb,
+                  s1, r1, s2a, r2a, s2b, r2b, s3, r3, s4, r4):
+    dp = lax.axis_index("dp")
+    core = lax.axis_index("fsdp")
+    z = dp // 16
+    y = (dp // 4) % 4
+    x = dp % 4
+
+    def at_x(i):
+        return (z * 16 + y * 4 + i, core)
+
+    def at_y(i):
+        return (z * 16 + i * 4 + x, core)
+
+    def at_z(i):
+        return (i * 16 + y * 4 + x, core)
+
+    barrier = pltpu.get_barrier_semaphore()
+    for d in range(1, 4):
+        for place in (at_x((x + d) % 4), at_y((y + d) % 4), at_z((z + d) % 4)):
+            pl.semaphore_signal(barrier, inc=1, device_id=place, device_id_type=MESH)
+    pl.semaphore_wait(barrier, 9)
+
+    def send(src, dst, ssem, rsem, place):
+        copy = pltpu.make_async_remote_copy(
+            src_ref=src, dst_ref=dst, send_sem=ssem, recv_sem=rsem, device_id=place, device_id_type=MESH
+        )
+        copy.start()
+        return copy
+
+    first = []
+    for d in range(1, 4):
+        to = (x + d) % 4
+        place = at_x(to)
+        first.append(send(hid, hidg.at[d], s1.at[0, d - 1], r1.at[0, d - 1], place))
+        first.append(send(rq.at[to], rqg.at[d], s1.at[1, d - 1], r1.at[1, d - 1], place))
+        first.append(send(gel, gelg.at[d], s1.at[2, d - 1], r1.at[2, d - 1], place))
+        first.append(send(rp.at[to], rpg.at[d], s1.at[3, d - 1], r1.at[3, d - 1], place))
+    hidg[0] = hid[...]
+    gelg[0] = gel[...]
+    rqg[0] = rq[x]
+    rpg[0] = rp[x]
+    for copy in first:
+        copy.wait()
+
+    second = []
+    for d in (1, 2, 3, 0):
+        zi = (z + d) % 4
+        lanes = pl.ds(pl.multiple_of(zi * TILE, TILE), TILE)
+        left = hidg[:, :, lanes].reshape(4 * ROWS, TILE)
+        prod = tn(left, rqg[...].reshape(4 * ROWS, QB)).astype(BF16).reshape(4, 96, QB)
+        ca[zi] = prod[:, :, 0:TILE]
+        cb[zi, :, :, 0:QB - TILE] = prod[:, :, TILE:QB]
+        left = gelg[:, :, lanes].reshape(4 * ROWS, TILE)
+        prod = tn(left, rpg[...].reshape(4 * ROWS, PB)).astype(BF16).reshape(4, 96, PB)
+        cb[zi, :, :, QB - TILE:QB - TILE + PB] = prod
+        cb[zi, :, :, QB - TILE + PB:TILE] = jnp.zeros((4, 96, 2 * TILE - QB - PB), BF16)
+        if d:
+            second.append(send(ca.at[zi], ra.at[d - 1], s2a.at[d - 1], r2a.at[d - 1], at_z(zi)))
+        for e in range(1, 4):
+            yi = (y + e) % 4
+            second.append(send(cb.at[zi, yi], rb.at[e - 1, zi], s2b.at[e - 1, d], r2b.at[e - 1, d], at_y(yi)))
+    for copy in second:
+        copy.wait()
+
+    def total(own, got):
+        return ((own.astype(F32) + got[0].astype(F32)) + (got[1].astype(F32) + got[2].astype(F32)))
+
+    sa[...] = total(ca[z], ra).astype(BF16)
+    sb[...] = total(cb[:, y], rb).astype(BF16)
+    third = []
+    for d in range(1, 4):
+        yi = (y + d) % 4
+        zi = (z + d) % 4
+        third.append(send(sa.at[yi], ta.at[d - 1], s3.at[0, d - 1], r3.at[0, d - 1], at_y(yi)))
+        third.append(send(sb.at[zi], tb.at[d - 1], s3.at[1, d - 1], r3.at[1, d - 1], at_z(zi)))
+    for copy in third:
+        copy.wait()
+    fa[...] = total(sa[y], ta).reshape(4, 24, TILE)
+    fb[...] = total(sb[z], tb).reshape(4, 24, TILE)
+    fourth = []
+    for d in range(1, 4):
+        xi = (x + d) % 4
+        fourth.append(send(fa.at[xi], ga.at[x], s4.at[0, d - 1], r4.at[0, d - 1], at_x(xi)))
+        fourth.append(send(fb.at[xi], gb.at[x], s4.at[1, d - 1], r4.at[1, d - 1], at_x(xi)))
+    ga[x] = fa[x]
+    gb[x] = fb[x]
+    for copy in fourth:
+        copy.wait()
+    for i in range(4):
+        a = ga[i][0:22, :]
+        b = gb[i][0:22, :]
+        for j in range(6):
+            head = 6 * i + j
+            lo = HD * j
+            hi = lo + HD
+            if hi <= TILE:
+                piece = a[:, lo:hi]
+            elif lo >= TILE:
+                piece = b[:, lo - TILE:hi - TILE]
+            else:
+                piece = jnp.concatenate([a[:, lo:TILE], b[:, 0:hi - TILE]], axis=1)
+            oq[head // 8, :, (head % 8) * HD:(head % 8) * HD + HD] = piece
+        op[:, PB * i:PB * i + PB] = b[:, QB - TILE:QB - TILE + PB]
+
+
+def run_weight(hid, gel, rq, rp):
+    vm = pl.BlockSpec(memory_space=pltpu.VMEM)
+    V = pltpu.VMEM
+    S = pltpu.SemaphoreType.DMA
+    return pl.pallas_call(
+        weight_kernel,
+        out_shape=(jax.ShapeDtypeStruct((3, 22, HALF), F32), jax.ShapeDtypeStruct((22, HALF), F32)),
+        in_specs=[vm] * 4,
+        out_specs=(vm, vm),
+        scratch_shapes=[
+            V((4, ROWS, PADW), BF16), V((4, ROWS, PADW), BF16), V((4, ROWS, QB), BF16), V((4, ROWS, PB), BF16),
+            V((4, 4, 96, TILE), BF16), V((4, 4, 96, TILE), BF16),
+            V((3, 4, 96, TILE), BF16), V((3, 4, 96, TILE), BF16),
+            V((4, 96, TILE), BF16), V((4, 96, TILE), BF16), V((3, 96, TILE), BF16), V((3, 96, TILE), BF16),
+            V((4, 24, TILE), F32), V((4, 24, TILE), F32), V((4, 24, TILE), F32), V((4, 24, TILE), F32),
+            S((4, 3)), S((4, 3)), S((3,)), S((3,)), S((3, 4)), S((3, 4)), S((2, 3)), S((2, 3)), S((2, 3)), S((2, 3)),
+        ],
+        compiler_params=pltpu.CompilerParams(
+            collective_id=1, has_side_effects=True, vmem_limit_bytes=60 * 1024 * 1024
+        ),
+    )(hid, gel, rq, rp)
+
+
+def spread_table():
+    table = np.zeros((D, PADW), np.float32)
+    cols = np.arange(D)
+    table[cols, (cols // 22) * 24 + cols % 22] = 1.0
+    return table
+
+
 def per_device(
     tokens, vis_index, owner, enc_gain, enc_qkv, enc_proj, to_decoder, mask_token, dec_gain1,
     dec_qkv, dec_proj, dec_gain2, dec_fc1, dec_fc2, cotangent,
@@ -364,13 +506,13 @@
         dec_gain1[None], dec_gain2[None], wt, enc_proj, to_decoder, dec_qkv, dec_proj,
         dec_fc1, dec_fc2, cotangent[0], jnp.asarray(position_rows()),
     )
-    qkv_term = jnp.dot(hidden.T, gqkv, preferred_element_type=F32).reshape(D, 3, HALF)
-    proj_term = jnp.dot(mixed.T, gel, preferred_element_type=F32)
-    return (
-        gtok[None],
-        lax.psum_scatter(qkv_term, "dp", scatter_dimension=0, tiled=True),
-        lax.psum_scatter(proj_term, "dp", scatter_dimension=1, tiled=True),
-    )
+    spread = jnp.asarray(spread_table(), BF16)
+    hid_pad = jnp.dot(hidden, spread)
+    gel_pad = jnp.dot(gel, spread)
+    rq = jnp.transpose(gqkv.reshape(ROWS, 4, QB), (1, 0, 2))
+    rp = jnp.transpose(mixed.reshape(ROWS, 4, PB), (1, 0, 2))
+    gq, gp = run_weight(hid_pad, gel_pad, rq, rp)
+    return gtok[None], jnp.transpose(gq, (1, 0, 2)), jnp.transpose(gp)
 
 
 def solution(mesh):

time: 380 us -> 203 us (0.53)
  blocking collectives: 209 us -> 0 us
  Pallas kernels: 79.8 us -> 172 us
  starting transfers between devices: 30.1 us -> 0 us
  between operations: 15.5 us -> 0.71 us
  local copies, waits for them, and re-layouts: 27.3 us -> 17.1 us
  waiting for transfers between devices: 5.35 us -> 0 us
    unnamed x1 -> x0, blocking collectives: 209 us -> none
    pallas_call x0 -> x1, Pallas kernels: none -> 92.6 us  [run_weight(): pl.pallas_call(weight_kernel, out_shape=(jax.ShapeDtypeStruct((3, 22, HAL...]
    unnamed x7 -> x0, starting transfers between devices: 30.1 us -> none
    reshape x1 -> x4, local copies, waits for them, and re-layouts: 13.7 us -> 5.32 us  [the longest x2 3.35 us: per_device(): rq = jnp.transpose(gqkv.reshape(ROWS, 4, QB), (1, 0, 2))]
    unnamed x8 -> x0, waiting for transfers between devices: 5.35 us -> none
  transfers between devices with their start and end apart: 7 -> 0, of which waited for: 2 -> 0; matrix products, arithmetic and copies ran while one was open for 57% -> 0% of each run, Pallas kernels for 0% -> 0%
where the time goes in v2:
time: 203 us; the launch traced here: 201 us
  Pallas kernels  172 us (85%)
  local copies, waits for them, and re-layouts  17.1 us (8%)
  matrix products  7.97 us (4%)
  other arithmetic  2.48 us (1%)
    pallas_call x1, Pallas kernels, run_weight(): pl.pallas_call(weight_kernel, out_shape=(jax.ShapeDtypeStruct((3, 22, HAL...  92.6 us
    pallas_call x1, Pallas kernels, run_main(): pl.pallas_call(main_kernel, out_shape=(jax.ShapeDtypeStruct((VIS, HALF),...  79.8 us
    unnamed x10, local copies, waits for them, and re-layouts  4.51 us

profile of v2, /device:TPU:96, one launch (start us, length us, event | category | flops | bytes accessed | tf_op | source)
XLA Modules:
  0.0 200.6 jit_solution(16414105050081505840)
XLA Ops:
  0.6 0.7 compare_convert_fusion
  1.4 0.3 reduce-window.6
  1.6 0.2 slice_reduce_fusion
  1.8 0.2 reduce-window.9
  2.0 0.1 broadcast_bitcast_fusion
  2.1 1.3 compare_select_fusion.rank
  3.4 1.2 pad_bitcast_fusion
  4.7 0.8 copy.21.visc
  5.4 1.3 broadcast_in_dim.17.genc
  6.7 1.3 broadcast_in_dim.18.maskt
  7.9 1.2 broadcast_in_dim.19.gain1
  9.2 1.3 broadcast_in_dim.20.gain2
  10.4 79.8 %shard_map.184 = (f32[157,704]{1,0:T(8,128)}, bf16[160,1408]{1,0:T(8,128)(2,1)}, bf16[160,2112]{1,0:T(8,128)(2,1)}, bf16[160,704]{1,0:T(8,128)(2,1)}, bf16[160,1408]{1,0:T(8,128)(2,1)}) custom-call(bf16[157,704]{1,0:T(8,128)(2,1)} %bitcast.37, s32[1,160]{1,0:T(1,128)} %get-tuple-element.24.visr, s32[160,1]{1,0:T(8,128)} %copy.21.visc, ...), custom_call_target="tpu_custom_call" | custom-call | tf_op jit(solution)/shard_map/pallas_call | solution.py:335
  90.2 0.0 copy-start.2
  90.3 2.4 %reshape.65 = bf16[160,4,528]{2,1,0:T(4,128)(2,1)S(1)} reshape(bf16[160,2112]{1,0:T(8,128)(2,1)} %get-tuple-element.13) | data formatting | bytes 1351680 | tf_op jit(solution)/shard_map/reshape | solution.py:512
  92.6 0.0 copy-start.1
  92.6 1.0 copy.31
  93.6 1.2 reshape.66
  94.8 0.8 copy.32
  95.6 0.0 copy-done.2
  95.6 4.0 %fusion.1.hid = bf16[160,1536]{1,0:T(8,128)(2,1)} fusion(bf16[160,1408]{1,0:T(8,128)(2,1)S(1)} %copy-done.2, bf16[1408,1536]{1,0:T(8,128)(2,1)} %constant.18.clone), kind=kOutput, calls=%fused_computation.13 | convolution fusion | flops 692060160 | bytes 5267456 | tf_op jit(solution)/shard_map/dot_general | solution.py:510
  99.6 0.0 copy-start
  99.6 0.0 copy-done.1
  99.6 4.0 %fusion.2.gel = bf16[160,1536]{1,0:T(8,128)(2,1)} fusion(bf16[160,1408]{1,0:T(8,128)(2,1)S(1)} %copy-done.1, bf16[1408,1536]{1,0:T(8,128)(2,1)} %constant.18.clone), kind=kOutput, calls=%fused_computation.14 | convolution fusion | flops 692060160 | bytes 5267456 | tf_op jit(solution)/shard_map/dot_general | solution.py:511
  103.6 92.6 %shard_map.185 = (f32[3,22,704]{2,1,0:T(8,128)}, f32[22,704]{1,0:T(8,128)}) custom-call(bf16[160,1536]{1,0:T(8,128)(2,1)} %fusion.1.hid, bf16[160,1536]{1,0:T(8,128)(2,1)} %fusion.2.gel, bf16[4,160,528]{2,1,0:T(8,128)(2,1)} %bitcast.33, bf16[4,160,176]{2,1,0:T(8,128)(2,1)} %bitcast.34), custom_call_target="tpu_custom_call" | custom-call | tf_op jit(solution)/shard_map/pallas_call | solution.py:469
  196.2 0.0 copy-done
  196.2 1.3 copy.24
  197.5 1.6 copy.35
  199.1 1.5 copy.36
  (3 shorter events, 0.0 us)
Async XLA Ops:
  90.2 5.4 %copy-start.2 = (bf16[160,1408]{1,0:T(8,128)(2,1)S(1)}, bf16[160,1408]{1,0:T(8,128)(2,1)}, u32[]{:S(2)}) copy-start(bf16[160,1408]{1,0:T(8,128)(2,1)} %get-tuple-element.11) | copy-start | bytes 1351684
  92.6 6.9 %copy-start.1 = (bf16[160,1408]{1,0:T(8,128)(2,1)S(1)}, bf16[160,1408]{1,0:T(8,128)(2,1)}, u32[]{:S(2)}) copy-start(bf16[160,1408]{1,0:T(8,128)(2,1)} %get-tuple-element.12) | copy-start | bytes 1351684
  99.6 96.6 %copy-start = (f32[157,704]{1,0:T(8,128)S(1)}, f32[157,704]{1,0:T(8,128)}, u32[]{:S(2)}) copy-start(f32[157,704]{1,0:T(8,128)} %get-tuple-element.10) | copy-start | bytes 1326340
